TPU v7x, 256 devices: a whole 4x4x8 slice. The times are simulated.
256 devices in a mesh: head: 8 (over z_hi, core), tm: 8 (over x, z_lo), height: 4 (over y).
Axes of the slice: x: 4, y: 4, z: 8 (z_hi: 4, z_lo: 2; z = z_hi * 2 + z_lo), core: 2. Of those that a mesh axis runs over, the one named last changes fastest.
Arguments:
- queries: bfloat16 [32, 24, 16, 3072], P('tm', 'height', None, 'head'), may hold values from -6 to 6
- key_tokens: bfloat16 [32, 24, 16, 3072], P('tm', 'height', None, 'head'), may hold values from -6 to 6
- value_tokens: bfloat16 [32, 24, 16, 3072], P('tm', 'height', None, 'head'), may hold values from -6 to 6
- tile_mask: int32 [64, 64], replicated, may hold values from 0 to 1, as said below
Outputs:
- attended: bfloat16 [32, 24, 16, 3072], P('tm', 'height', None, 'head')
Inputs may be any that keep to these rules, and one draw needn't show every extreme that they name: tile_mask[a, b] is 1 only where key tile b lies at most one tile row and at most two tile columns away from query tile a, at any distance in frames; tile_mask[a, a] is 1. Other pairs inside that window may be 0.
All inputs are finite; a program needn't handle non-finite values.
Results may differ from a plain program's by a relative error of at most 0.024.
Values may be sent and summed in bfloat16 or wider, within the bound.
A program may use at most 64 MiB of HBM per device.

v0:
```python
import jax
import jax.numpy as jnp
from jax import lax
from jax.sharding import PartitionSpec as P

HEAD_DIM = 128
TILE_T = 4
TILE_R = 6
TILE_C = 8


NEG_FILL = -1e30


def frame_block(frame_count, per_frame):
    best_size = 1
    for option in range(1, frame_count + 1):
        if frame_count % option == 0 and option * per_frame <= 1024:
            best_size = option
    return best_size


def key_tiles(frame_tile, row_first, row_count, col_count, row_tiles, col_tiles):
    global_row = row_first[:, None] + jnp.arange(row_count, dtype=jnp.int32)[None, :]
    inside = (global_row >= 0) & (global_row < row_tiles * TILE_R)
    row_tile = jnp.maximum(global_row, 0) // TILE_R
    col_tile = jnp.arange(col_count, dtype=jnp.int32) // TILE_C
    tile_ids = (frame_tile[:, None] * row_tiles + row_tile)[:, :, None] * col_tiles + col_tile[
        None, None, :
    ]
    return jnp.where(inside[:, :, None], tile_ids, -1).reshape(-1)


def live_pairs(tile_ids, tile_table, select):
    onehot = (
        tile_ids[:, None] == jnp.arange(tile_table.shape[1], dtype=jnp.int32)[None, :]
    ).astype(jnp.float32)
    tile_live = jnp.einsum("nt,kt->nk", tile_table, onehot, precision=lax.Precision.HIGHEST)
    return jnp.dot(select, tile_live, precision=lax.Precision.HIGHEST) > 0.5


def query_tables(
    mask_table, time_first, row_first, row_tiles, col_tiles, frame_count, row_count, col_count
):
    per_time = frame_count // TILE_T
    per_row = row_count // TILE_R
    local_ids = jnp.arange(per_time * per_row * col_tiles, dtype=jnp.int32)
    global_ids = (
        (time_first + local_ids // (per_row * col_tiles)) * row_tiles
        + row_first
        + local_ids // col_tiles % per_row
    ) * col_tiles + local_ids % col_tiles
    onehot = (
        global_ids[:, None] == jnp.arange(mask_table.shape[0], dtype=jnp.int32)[None, :]
    ).astype(jnp.float32)
    tile_table = jnp.dot(onehot, mask_table, precision=lax.Precision.HIGHEST)
    frame_part = jnp.arange(frame_count, dtype=jnp.int32) // TILE_T
    row_part = jnp.arange(row_count, dtype=jnp.int32) // TILE_R
    col_part = jnp.arange(col_count, dtype=jnp.int32) // TILE_C
    query_local = (
        (frame_part[:, None, None] * per_row + row_part[None, :, None]) * col_tiles
        + col_part[None, None, :]
    ).reshape(-1)
    select = (query_local[:, None] == local_ids[None, :]).astype(jnp.float32)
    return (tile_table, select)


def update(carry_state, query_mat, key_block, value_block, live_mask):
    peak_now, total_now, sum_now = carry_state
    scores = jnp.einsum(
        "qhd,khd->qhk", query_mat, key_block, preferred_element_type=jnp.float32
    ) * query_mat.shape[2] ** (-0.5)
    scores = jnp.where(live_mask[:, None, :], scores, NEG_FILL)
    peak_new = jnp.maximum(peak_now, jnp.max(scores, axis=2))
    raw_weights = jnp.where(live_mask[:, None, :], jnp.exp(scores - peak_new[:, :, None]), 0.0)
    factor = jnp.exp(peak_now - peak_new)
    total_new = total_now * factor + jnp.sum(raw_weights, axis=2)
    sum_new = sum_now * factor[:, :, None] + jnp.einsum(
        "qhk,khd->qhd",
        raw_weights.astype(jnp.bfloat16),
        value_block,
        preferred_element_type=jnp.float32,
    )
    return (peak_new, total_new, sum_new)


def attend_frames(
    carry_state, query_mat, tile_table, select, band, frame_tile, row_first, row_tiles, col_tiles
):
    frame_count = band.shape[1]
    band_rows = band.shape[2]
    band_cols = band.shape[3]
    head_count = query_mat.shape[1]
    group_size = frame_block(frame_count, band_rows * band_cols)

    def visit(step_index, state_now):
        begin = step_index * group_size
        section = lax.dynamic_slice_in_dim(band, begin, group_size, 1)
        tile_ids = key_tiles(
            lax.dynamic_slice_in_dim(frame_tile, begin, group_size, 0),
            lax.dynamic_slice_in_dim(row_first, begin, group_size, 0),
            band_rows,
            band_cols,
            row_tiles,
            col_tiles,
        )
        live_mask = live_pairs(tile_ids, tile_table, select)
        key_block = section[0].reshape(-1, head_count, HEAD_DIM)
        value_block = section[1].reshape(-1, head_count, HEAD_DIM)
        return update(state_now, query_mat, key_block, value_block, live_mask)

    return lax.fori_loop(0, frame_count // group_size, visit, carry_state)


def shards(queries, key_tokens, value_tokens, tile_mask):
    frame_count, row_count, col_count, chan_count = queries.shape
    head_count = chan_count // HEAD_DIM
    height_size = lax.axis_size("height")
    tm_index = lax.axis_index("tm")
    height_index = lax.axis_index("height")
    row_tiles = row_count * height_size // TILE_R
    col_tiles = col_count // TILE_C
    mask_table = tile_mask.astype(jnp.float32)
    tok_count = frame_count * row_count * col_count
    query_mat = queries.reshape(tok_count, head_count, HEAD_DIM)
    paired = jnp.stack([key_tokens, value_tokens])
    start_state = (
        jnp.full((tok_count, head_count), NEG_FILL, jnp.float32),
        jnp.zeros((tok_count, head_count), jnp.float32),
        jnp.zeros((tok_count, head_count, HEAD_DIM), jnp.float32),
    )
    own_time = tm_index * (frame_count // TILE_T)
    own_row = height_index * (row_count // TILE_R)
    tile_table, select = query_tables(
        mask_table, own_time, own_row, row_tiles, col_tiles, frame_count, row_count, col_count
    )
    gathered = lax.all_gather(paired, ("tm", "height"), axis=1, tiled=True)
    position = jnp.arange(gathered.shape[1], dtype=jnp.int32)
    source = position // frame_count
    frame_tile = (source // height_size * frame_count + position % frame_count) // TILE_T
    row_first = source % height_size * row_count
    final_state = attend_frames(
        start_state,
        query_mat,
        tile_table,
        select,
        gathered,
        frame_tile,
        row_first,
        row_tiles,
        col_tiles,
    )
    result = final_state[2] / final_state[1][:, :, None]
    return result.astype(jnp.bfloat16).reshape(frame_count, row_count, col_count, chan_count)


def solution(mesh):
    return jax.shard_map(
        shards,
        mesh=mesh,
        in_specs=(
            P("tm", "height", None, "head"),
            P("tm", "height", None, "head"),
            P("tm", "height", None, "head"),
            P(),
        ),
        out_specs=P("tm", "height", None, "head"),
        check_vma=False,
    )
```

profile of v0, /device:TPU:1, one launch (start us, length us, event | category | flops | bytes accessed | tf_op | source)
XLA Modules:
  0.0 575.4 jit_solution(13512606870750288853)
XLA Ops:
  13.5 214.4 %all-gather.2.cloned.1.call-done = bf16[2,128,6,16,384]{4,3,2,1,0:T(8,128)(2,1)} async-done(((bf16[2,4,6,16,384]{4,3,2,1,0:T(8,128)(2,1)}), bf16[2,128,6,16,384]{4,3,2,1,0:T(8,128)(2,1)}) %all-gather.2.cloned.1.call-update) | async-done | bytes 18874384 | tf_op jit(solution)/shard_map/all_gather | solution.py:137
  227.9 338.3 %while.21 = (s32[]{:T(128)}, f32[384,3]{0,1:T(4,128)S(1)}, f32[384,3]{0,1:T(4,128)}, f32[384,3,128]{0,2,1:T(8,128)}, s32[128]{0:T(128)}, /*index=5*/s32[128]{0:T...) while((s32[]{:T(128)}, f32[384,3]{0,1:T(4,128)S(1)}, ...), condition=%wide.region_3.4_spmd.clone, body=%wide.region_0.3_spmd.clone.sunk | while | flops 473540096 | bytes 19270692 | solution.py:112
  236.5 2.7 fusion.72
  245.0 3.2 fusion.75
  256.8 2.7 fusion.72
  266.0 3.4 fusion.75
  278.0 2.7 fusion.72
  287.2 3.4 fusion.75
  299.2 2.7 fusion.72
  308.4 3.4 fusion.75
  320.4 2.7 fusion.72
  329.6 3.4 fusion.75
  341.6 2.7 fusion.72
  350.8 3.4 fusion.75
  372.0 3.4 fusion.75
  393.2 3.4 fusion.75
  414.4 3.4 fusion.75
  435.6 3.4 fusion.75
  456.8 3.4 fusion.75
  478.0 3.4 fusion.75
  499.2 3.4 fusion.75
  520.4 3.4 fusion.75
  541.6 3.4 fusion.75
  562.8 3.4 fusion.75
  (286 shorter events, 276.4 us)
Async XLA Ops:
  6.5 221.4 %all-gather.2.cloned.1.call-start = ((), (), s32[]{:S(2)}) async-start(), calls=%async_computation | async-start | bytes 19464192 | tf_op jit(solution)/shard_map/all_gather | solution.py:137
Sparse Core Ops, SparseCore 0:
  9.1 218.7 all-gather.1
where the time goes:
time: 581 us; the launch traced here: 575 us
  waiting for transfers between devices  214 us (37%)
  matrix products  159 us (27%)
  local copies, waits for them, and re-layouts  109 us (19%)
  other arithmetic  79.6 us (14%)
  between operations  13.4 us (2%)
    all_gather x1, waiting for transfers between devices, shards(): gathered = lax.all_gather(paired, ('tm', 'height'), axis=1, tiled=True)  214 us
    dot_general x16, matrix products, update(): jnp.einsum('qhk,khd->qhd', raw_weights.astype(jnp.bfloat16), value_block,...  54.3 us
    dot_general x16, matrix products, update(): jnp.einsum('qhd,khd->qhk', query_mat, key_block, preferred_element_type=j...  43.8 us
    dot_general x16, matrix products, live_pairs(): return jnp.dot(select, tile_live, precision=lax.Precision.HIGHEST) > 0.5  41.9 us
    squeeze x16, local copies, waits for them, and re-layouts, visit(): value_block = section[1].reshape(-1, head_count, HEAD_DIM)  41.8 us
    slice x16, local copies, waits for them, and re-layouts, visit(): value_block = section[1].reshape(-1, head_count, HEAD_DIM)  34.9 us
    reduce_sum x16, other arithmetic, update(): total_new = total_now * factor + jnp.sum(raw_weights, axis=2)  29.7 us
    add x16, other arithmetic, update(): total_new = total_now * factor + jnp.sum(raw_weights, axis=2)  20.3 us
  transfers between devices with their start and end apart: 1, of which 1 were waited for; matrix products, arithmetic and copies ran while one was open for 1% of the time, Pallas kernels for 0%

commit v1 on v0

v1 whole, which is shorter than its diff:
```python
import functools

import jax
import jax.numpy as jnp
from jax import lax
from jax.experimental import pallas as pl
from jax.experimental.pallas import tpu as pltpu
from jax.sharding import PartitionSpec as P

HEAD_DIM = 128
TILE_T = 4
TILE_R = 6
TILE_C = 8
MESH = pl.DeviceIdType.MESH
NEG_FILL = -1e30
EXP_SCALE = HEAD_DIM**-0.5 * 1.4426950408889634
NT = (((1,), (1,)), ((), ()))
COL_BLOCKS = (256, 256, 256, 256, 128)
OFFSETS = (0, 3, 1, 2)


def kernel(
    heads, tok,
    q_in, k_in, v_in, mask_ref, out_ref,
    qbuf, kbuf, vbuf, vt, bias, peak, acc, osend, orecv,
    swap_s, swap_r, x_s, x_r, d_s, d_r, q_s, q_r, o_s, o_r,
):
    head = lax.axis_index("head")
    tm = lax.axis_index("tm")
    y = lax.axis_index("height")
    nx = lax.axis_size("tm") // 2
    ny = lax.axis_size("height")
    zh, c = lax.div(head, 2), lax.rem(head, 2)
    x, z = lax.div(tm, 2), lax.rem(tm, 2)
    same = c == z
    inner = jnp.logical_and(y > 0, y < ny - 1)
    own_t = 2 * x + c

    def dev(h, t, r):
        return {"head": h, "tm": t, "height": r}

    partner_head, partner_tm = 2 * zh + z, 2 * x + c
    partner = dev(partner_head, partner_tm, y)
    right = dev(head, 2 * lax.rem(x + 1, nx) + z, y)
    left = dev(head, 2 * lax.rem(x + nx - 1, nx) + z, y)
    sibling = dev(2 * zh + 1 - c, tm, y)

    def remote(src, dst, ssem, rsem, to):
        return pltpu.make_async_remote_copy(
            src_ref=src, dst_ref=dst, send_sem=ssem, recv_sem=rsem, device_id=to, device_id_type=MESH
        )

    barrier = pltpu.get_barrier_semaphore()

    def greet(to):
        pl.semaphore_signal(barrier, inc=1, device_id=to, device_id_type=MESH)

    greet(right)
    greet(left)
    greet(sibling)
    pl.when(y > 0)(lambda: greet(dev(head, tm, y - 1)))
    pl.when(y < ny - 1)(lambda: greet(dev(head, tm, y + 1)))

    @pl.when(jnp.logical_not(same))
    def _():
        greet(partner)
        pl.when(y > 0)(lambda: greet(dev(partner_head, partner_tm, y - 1)))
        pl.when(y < ny - 1)(lambda: greet(dev(partner_head, partner_tm, y + 1)))

    for h in range(heads):
        vt[h] = v_in[:, h * HEAD_DIM : (h + 1) * HEAD_DIM].astype(jnp.float32).T.astype(jnp.bfloat16)
        for t in range(2 * nx):
            vbuf[h, t, HEAD_DIM:] = jnp.ones((16, tok), jnp.bfloat16)
    row_tiles = ny
    tiles = mask_ref.shape[0]
    key_row = lax.broadcasted_iota(jnp.int32, (4 * nx, tiles), 0)
    key_tile = (lax.shift_right_logical(key_row, 1) * row_tiles + y) * 2 + (key_row & 1)
    key_hot = (lax.broadcasted_iota(jnp.int32, (4 * nx, tiles), 1) == key_tile).astype(jnp.bfloat16)
    by_key = lax.dot_general(
        key_hot, mask_ref[...].astype(jnp.float32).astype(jnp.bfloat16), NT, preferred_element_type=jnp.float32
    ).astype(jnp.bfloat16)
    col = lax.broadcasted_iota(jnp.int32, (1, tok), 1)
    col_tile = lax.shift_right_logical(col, 3) & 1
    tile_id = lax.broadcasted_iota(jnp.int32, (tiles, tok), 0)
    q_rows = (y, jnp.where(y > 0, y - 1, y + 1), y + 1)
    for b in range(3):
        q_tile = (own_t * row_tiles + q_rows[b]) * 2 + col_tile
        q_hot = (tile_id == q_tile).astype(jnp.bfloat16)
        live = jnp.dot(by_key, q_hot, preferred_element_type=jnp.float32)
        fill = (1.0 - live) * NEG_FILL
        for i in range(4 * nx):
            bias[i // 4, i // 2 % 2, 8 * (i % 2) : 8 * (i % 2) + 8, b * tok : (b + 1) * tok] = jnp.broadcast_to(
                fill[i : i + 1], (8, tok)
            )

    per_edge = (y > 0).astype(jnp.int32) + (y < ny - 1).astype(jnp.int32)
    pl.semaphore_wait(barrier, 3 + per_edge + jnp.where(same, 0, 1 + per_edge))

    def swap_parts(h):
        cols = slice(h * HEAD_DIM, (h + 1) * HEAD_DIM)
        return (
            (k_in.at[:, cols], lambda t: kbuf.at[h, t]),
            (q_in.at[:, cols], lambda t: qbuf.at[h, pl.ds(0, tok)]),
            (vt.at[h], lambda t: vbuf.at[h, t, pl.ds(0, HEAD_DIM)]),
        )

    for h in range(heads):
        for i, (src, dst) in enumerate(swap_parts(h)):

            @pl.when(same)
            def _(src=src, dst=dst, h=h, i=i):
                pltpu.make_async_copy(src, dst(own_t), swap_r.at[h, i]).start()

            @pl.when(jnp.logical_not(same))
            def _(src=src, dst=dst, h=h, i=i):
                remote(src, dst(2 * x + z), swap_s.at[h, i], swap_r.at[h, i], partner).start()

    def swap_wait(h, i):
        src = (kbuf.at[h, own_t], qbuf.at[h, pl.ds(0, tok)], vbuf.at[h, own_t, pl.ds(0, HEAD_DIM)])[i]

        @pl.when(same)
        def _():
            pltpu.make_async_copy(src, src, swap_r.at[h, i]).wait()

        @pl.when(jnp.logical_not(same))
        def _():
            remote(src, src, swap_s.at[h, i], swap_r.at[h, i], partner).wait_recv()

    def slot(d):
        return 2 * lax.rem(x + OFFSETS[d], nx) + c

    def piece(h, kind, t):
        return kbuf.at[h, t] if kind == 0 else vbuf.at[h, t, pl.ds(0, HEAD_DIM)]

    def x_copy(h, direction, step, kind, d):
        ref = piece(h, kind, slot(d))
        return remote(
            ref, ref, x_s.at[h, direction, step], x_r.at[h, direction, step], right if direction == 0 else left
        )

    def d_copy(h, kind, d, mine=True):
        t = slot(d) if mine else 2 * lax.rem(x + OFFSETS[d], nx) + 1 - c
        ref = piece(h, kind, t)
        return remote(ref, ref, d_s.at[h, d, kind], d_r.at[h, d, kind], sibling)

    def q_copies(h, act):
        src = qbuf.at[h, pl.ds(0, tok)]

        @pl.when(y < ny - 1)
        def _():
            act(remote(src, qbuf.at[h, pl.ds(tok, tok)], q_s.at[h, 0], q_r.at[h, 0], dev(head, tm, y + 1)))

        @pl.when(y > 0)
        def _():
            at = pl.multiple_of(jnp.where(y > 1, 2 * tok, tok), tok)
            act(remote(src, qbuf.at[h, pl.ds(at, tok)], q_s.at[h, 1], q_r.at[h, 1], dev(head, tm, y - 1)))

    def q_wait(h):
        @pl.when(y > 0)
        def _():
            ref = qbuf.at[h, pl.ds(tok, tok)]
            remote(ref, ref, q_s.at[h, 0], q_r.at[h, 0], dev(head, tm, y - 1)).wait_recv()

        @pl.when(y < ny - 1)
        def _():
            at = pl.multiple_of(jnp.where(y > 0, 2 * tok, tok), tok)
            ref = qbuf.at[h, pl.ds(at, tok)]
            remote(ref, ref, q_s.at[h, 1], q_r.at[h, 1], dev(head, tm, y + 1)).wait_recv()

    def send_own(h):
        swap_wait(h, 0)
        x_copy(h, 0, 0, 0, 0).start()
        x_copy(h, 1, 0, 0, 0).start()
        d_copy(h, 0, 0).start()
        swap_wait(h, 1)
        q_copies(h, lambda copy: copy.start())
        swap_wait(h, 2)
        x_copy(h, 0, 1, 1, 0).start()
        x_copy(h, 1, 1, 1, 0).start()
        d_copy(h, 1, 0).start()

    def pass_on(h):
        x_copy(h, 0, 0, 0, 1).wait_recv()
        x_copy(h, 0, 2, 0, 1).start()
        d_copy(h, 0, 1).start()
        x_copy(h, 1, 0, 0, 2).wait_recv()
        d_copy(h, 0, 2).start()
        x_copy(h, 1, 1, 1, 2).wait_recv()
        x_copy(h, 1, 2, 1, 2).start()
        d_copy(h, 1, 2).start()
        x_copy(h, 0, 1, 1, 1).wait_recv()
        d_copy(h, 1, 1).start()

    def take_last(h):
        x_copy(h, 0, 2, 0, 3).wait_recv()
        d_copy(h, 0, 3).start()
        x_copy(h, 1, 2, 1, 3).wait_recv()
        d_copy(h, 1, 3).start()

    edges = [sum(COL_BLOCKS[:i]) for i in range(len(COL_BLOCKS) + 1)]
    blocks = len(COL_BLOCKS)

    def unit(h, d):
        d_copy(h, 0, d, False).wait_recv()
        d_copy(h, 1, d, False).wait_recv()
        first = d == 0
        bx = lax.rem(x + OFFSETS[d], nx)
        state = {}

        def scores(n):
            cols = slice(edges[n], edges[n + 1])
            halves = []
            for p in range(2):
                s = lax.dot_general(
                    kbuf[h, 2 * bx + p], qbuf[h, cols], NT, preferred_element_type=jnp.float32
                )
                halves.append(s.reshape(tok // 16, 16, -1) + bias[bx, p, :, cols][None])
            top = jnp.maximum(jnp.max(halves[0], axis=0), jnp.max(halves[1], axis=0))
            top = jnp.max(top, axis=0, keepdims=True)
            if not first:
                before = peak[:1, cols]
                top = jnp.maximum(before, top)
                state["fade", n] = jnp.exp2((before - top) * EXP_SCALE)
            peak[:1, cols] = top
            state["s", n] = halves
            state["top", n] = top

        def weigh(n):
            top = state["top", n]
            halves = [
                jnp.exp2((s - top[None]) * EXP_SCALE).reshape(tok, -1).astype(jnp.bfloat16)
                for s in state.pop(("s", n))
            ]
            state["w", n] = jnp.concatenate(halves, axis=0)

        def gather(n):
            cols = slice(edges[n], edges[n + 1])
            values = jnp.concatenate([vbuf[h, 2 * bx], vbuf[h, 2 * bx + 1]], axis=1)
            o = jnp.dot(values, state.pop(("w", n)), preferred_element_type=jnp.float32)
            acc[:, cols] = o if first else acc[:, cols] * state["fade", n] + o

        for n in range(blocks + 2):
            if n < blocks:
                scores(n)
            if n >= 2:
                gather(n - 2)
            if 1 <= n <= blocks:
                weigh(n - 1)

    def o_copies(h, act_remote, act_local=None):
        def far(b, row, at):
            return remote(
                osend.at[h, b], orecv.at[h, at], o_s.at[h, b], o_r.at[h, at], dev(partner_head, partner_tm, row)
            )

        if act_local is not None:

            @pl.when(same)
            def _():
                act_local(pltpu.make_async_copy(osend.at[h, 0], orecv.at[h, 1], o_r.at[h, 1]))

        @pl.when(jnp.logical_not(same))
        def _():
            act_remote(far(0, y, 1))

        act_remote(far(1, q_rows[1], jnp.where(y > 0, 2, 0)))
        pl.when(inner)(lambda: act_remote(far(2, y + 1, 0)))

    def finish(h):
        row = lax.broadcasted_iota(jnp.int32, (16, tok), 0)
        for b in range(3):
            cols = slice(b * tok, (b + 1) * tok)
            total = acc[HEAD_DIM : HEAD_DIM + 1, cols]
            osend[h, b, :HEAD_DIM] = (acc[:HEAD_DIM, cols] / total).astype(jnp.bfloat16)
            log = peak[:1, cols] * EXP_SCALE + jnp.log2(total)
            hi = log.astype(jnp.bfloat16).astype(jnp.float32)
            mid = (log - hi).astype(jnp.bfloat16).astype(jnp.float32)
            low = log - hi - mid
            osend[h, b, HEAD_DIM:] = jnp.where(row == 0, hi, jnp.where(row == 1, mid, low)).astype(jnp.bfloat16)
        o_copies(h, lambda copy: copy.start(), lambda copy: copy.start())

    def merge(h):
        def far(at, row):
            ref = orecv.at[h, at]
            remote(ref, ref, o_s.at[h, 0], o_r.at[h, at], dev(partner_head, partner_tm, row)).wait_recv()

        @pl.when(same)
        def _():
            pltpu.make_async_copy(osend.at[h, 0], orecv.at[h, 1], o_r.at[h, 1]).wait()

        pl.when(jnp.logical_not(same))(lambda: far(1, y))
        pl.when(y > 0)(lambda: far(0, y - 1))
        pl.when(y < ny - 1)(lambda: far(2, y + 1))
        there = (y > 0, None, y < ny - 1)
        logs, parts = [], []
        for at in range(3):
            tail = orecv[h, at, HEAD_DIM:].astype(jnp.float32)
            log = tail[0:1] + tail[1:2] + tail[2:3]
            part = orecv[h, at, :HEAD_DIM].astype(jnp.float32)
            if there[at] is not None:
                log = jnp.where(there[at], log, -3e38)
                part = jnp.where(there[at], part, 0.0)
            logs.append(log)
            parts.append(part)
        top = jnp.maximum(jnp.maximum(logs[0], logs[1]), logs[2])
        shares = [jnp.exp2(log - top) for log in logs]
        total = shares[0] + shares[1] + shares[2]
        result = sum(part * (share / total) for part, share in zip(parts, shares))
        out_ref[h] = result.T.astype(jnp.bfloat16)

    send_own(0)
    send_own(1)

    def one_head(h, carry):
        q_wait(h)
        unit(h, 0)
        pass_on(h)
        pl.when(h + 2 < heads)(lambda: send_own(h + 2))
        unit(h, 1)
        unit(h, 2)
        take_last(h)
        pl.when(h > 0)(lambda: merge(h - 1))
        unit(h, 3)
        finish(h)
        return carry

    lax.fori_loop(0, heads, one_head, 0)
    merge(heads - 1)

    def drain(h, carry):
        @pl.when(jnp.logical_not(same))
        def _():
            for i, (src, dst) in enumerate(
                ((kbuf.at[h, 0], 0), (qbuf.at[h, pl.ds(0, tok)], 0), (vt.at[h], 0))
            ):
                remote(src, src, swap_s.at[h, i], swap_r.at[h, i], partner).wait_send()

        for direction in range(2):
            x_copy(h, direction, 0, 0, 0).wait_send()
            x_copy(h, direction, 1, 1, 0).wait_send()
        x_copy(h, 0, 2, 0, 1).wait_send()
        x_copy(h, 1, 2, 1, 2).wait_send()
        for d in range(4):
            d_copy(h, 0, d).wait_send()
            d_copy(h, 1, d).wait_send()
        q_copies(h, lambda copy: copy.wait_send())
        o_copies(h, lambda copy: copy.wait_send())
        return carry

    lax.fori_loop(0, heads, drain, 0)


def solution(mesh):
    times = mesh.shape["tm"]

    def shards(queries, key_tokens, value_tokens, tile_mask):
        frames, rows, cols, chans = queries.shape
        tok = frames * rows * cols
        heads = chans // HEAD_DIM
        bf16, f32 = jnp.bfloat16, jnp.float32
        dma = pltpu.SemaphoreType.DMA
        vmem = pl.BlockSpec(memory_space=pltpu.VMEM)
        out = pl.pallas_call(
            functools.partial(kernel, heads, tok),
            out_shape=jax.ShapeDtypeStruct((heads, tok, HEAD_DIM), bf16),
            in_specs=[vmem] * 4,
            out_specs=vmem,
            scratch_shapes=[
                pltpu.VMEM((heads, 3 * tok, HEAD_DIM), bf16),
                pltpu.VMEM((heads, times, tok, HEAD_DIM), bf16),
                pltpu.VMEM((heads, times, HEAD_DIM + 16, tok), bf16),
                pltpu.VMEM((heads, HEAD_DIM, tok), bf16),
                pltpu.VMEM((times // 2, 2, 16, 3 * tok), f32),
                pltpu.VMEM((8, 3 * tok), f32),
                pltpu.VMEM((HEAD_DIM + 16, 3 * tok), f32),
                pltpu.VMEM((heads, 3, HEAD_DIM + 16, tok), bf16),
                pltpu.VMEM((heads, 3, HEAD_DIM + 16, tok), bf16),
                dma((heads, 3)), dma((heads, 3)),
                dma((heads, 2, 3)), dma((heads, 2, 3)),
                dma((heads, 4, 2)), dma((heads, 4, 2)),
                dma((heads, 2)), dma((heads, 2)),
                dma((heads, 3)), dma((heads, 3)),
            ],
            compiler_params=pltpu.CompilerParams(
                collective_id=0, has_side_effects=True, vmem_limit_bytes=48 * 2**20
            ),
        )(
            queries.reshape(tok, chans),
            key_tokens.reshape(tok, chans),
            value_tokens.reshape(tok, chans),
            tile_mask,
        )
        return jnp.transpose(out, (1, 0, 2)).reshape(frames, rows, cols, chans)

    return jax.shard_map(
        shards,
        mesh=mesh,
        in_specs=(
            P("tm", "height", None, "head"),
            P("tm", "height", None, "head"),
            P("tm", "height", None, "head"),
            P(),
        ),
        out_specs=P("tm", "height", None, "head"),
        check_vma=False,
    )
```

time: 581 us -> 51.6 us (0.09)
  waiting for transfers between devices: 214 us -> 0 us
  matrix products: 159 us -> 0 us
  local copies, waits for them, and re-layouts: 109 us -> 4.86 us
  other arithmetic: 79.6 us -> 0 us
  Pallas kernels: 0 us -> 46.5 us
  between operations: 13.4 us -> 0.02 us
    all_gather x1 -> x0, waiting for transfers between devices: 214 us -> none  [shards(): gathered = lax.all_gather(paired, ('tm', 'height'), axis=1, tiled=True)]
    dot_general x65 -> x0, matrix products: 159 us -> none  [the longest x16 54.3 us: update(): jnp.einsum('qhk,khd->qhd', raw_weights.astype(jnp.bfloat16), value_block,...]
    squeeze x32 -> x0, local copies, waits for them, and re-layouts: 57.8 us -> none  [the longest x16 41.8 us: visit(): value_block = section[1].reshape(-1, head_count, HEAD_DIM)]
    pallas_call x0 -> x1, Pallas kernels: none -> 46.5 us  [shards(): pl.pallas_call(functools.partial(kernel, heads, tok), out_shape=jax.Shape...]
    slice x16 -> x0, local copies, waits for them, and re-layouts: 34.9 us -> none  [visit(): value_block = section[1].reshape(-1, head_count, HEAD_DIM)]
    reduce_sum x16 -> x0, other arithmetic: 29.7 us -> none  [update(): total_new = total_now * factor + jnp.sum(raw_weights, axis=2)]
    add x18 -> x0, other arithmetic: 20.3 us -> none  [the longest x16 20.3 us: update(): total_new = total_now * factor + jnp.sum(raw_weights, axis=2)]
    mul x33 -> x0, other arithmetic: 12.3 us -> none  [the longest x16 10.9 us: key_tiles(): frame_tile[:, None] * row_tiles + row_tile]
  transfers between devices with their start and end apart: 1 -> 0, of which waited for: 1 -> 0; matrix products, arithmetic and copies ran while one was open for 1% -> 0% of each run, Pallas kernels for 0% -> 0%
where the time goes in v1:
time: 51.6 us; the launch traced here: 51.4 us
  Pallas kernels  46.5 us (90%)
  local copies, waits for them, and re-layouts  4.86 us (9%)
    pallas_call x1, Pallas kernels, shards(): pl.pallas_call(functools.partial(kernel, heads, tok), out_shape=jax.Shape...  46.5 us
    unnamed x8, local copies, waits for them, and re-layouts  3.64 us

profile of v1, /device:TPU:1, one launch (start us, length us, event | category | flops | bytes accessed | tf_op | source)
XLA Modules:
  0.0 51.4 jit_solution(2935438677061458094)
XLA Ops:
  0.0 0.0 copy-start
  0.0 1.0 %copy-done = bf16[4,6,16,384]{3,2,1,0:T(8,128)(2,1)S(1)} copy-done((bf16[4,6,16,384]{3,2,1,0:T(8,128)(2,1)S(1)}, bf16[4,6,16,384]{3,2,1,0:T(8,128)(2,1)}, u32[]{:S(2)}) %copy-start) | copy-done | bytes 294936
  1.0 0.0 copy-start.1
  1.0 1.0 %copy-done.1 = bf16[4,6,16,384]{3,2,1,0:T(8,128)(2,1)S(1)} copy-done((bf16[4,6,16,384]{3,2,1,0:T(8,128)(2,1)S(1)}, bf16[4,6,16,384]{3,2,1,0:T(8,128)(2,1)}, u32[]{:S(2)}) %copy-start.1) | copy-done | bytes 294936
  1.9 0.0 copy-start.2
  1.9 1.0 %copy-done.2 = bf16[4,6,16,384]{3,2,1,0:T(8,128)(2,1)S(1)} copy-done((bf16[4,6,16,384]{3,2,1,0:T(8,128)(2,1)S(1)}, bf16[4,6,16,384]{3,2,1,0:T(8,128)(2,1)}, u32[]{:S(2)}) %copy-start.2) | copy-done | bytes 294936
  2.9 0.0 copy-start.3
  2.9 0.8 %copy-done.3 = s32[64,64]{1,0:T(8,128)S(1)} copy-done((s32[64,64]{1,0:T(8,128)S(1)}, s32[64,64]{1,0:T(8,128)}, u32[]{:S(2)}) %copy-start.3) | copy-done | bytes 16408
  3.6 46.5 %shard_map.46 = bf16[3,384,128]{2,1,0:T(8,128)(2,1)S(1)} custom-call(bf16[384,384]{1,0:T(8,128)(2,1)S(1)} %bitcast.5, bf16[384,384]{1,0:T(8,128)(2,1)S(1)} %bitcast.6, bf16[384,384]{1,0:T(8,128)(2,1)S(1)} %bitcast.7, s32[64,64]{1,0:T(8,128)S(1)} %copy-done.3), custom_call_target="tpu_custom_call" | custom-call | tf_op jit(solution)/shard_map/pallas_call | solution.py:363
  50.2 0.3 copy.5
  50.4 1.0 %reshape.15 = bf16[4,6,16,384]{3,2,1,0:T(8,128)(2,1)} reshape(bf16[384,3,128]{2,1,0:T(4,128)(2,1)S(1)} %copy.5) | data formatting | bytes 589824 | tf_op jit(solution)/shard_map/reshape | solution.py:393
Async XLA Ops:
  0.0 1.0 %copy-start = (bf16[4,6,16,384]{3,2,1,0:T(8,128)(2,1)S(1)}, bf16[4,6,16,384]{3,2,1,0:T(8,128)(2,1)}, u32[]{:S(2)}) copy-start(bf16[4,6,16,384]{3,2,1,0:T(8,128)(2,1)} %param.4) | copy-start | bytes 884740
  1.0 1.0 %copy-start.1 = (bf16[4,6,16,384]{3,2,1,0:T(8,128)(2,1)S(1)}, bf16[4,6,16,384]{3,2,1,0:T(8,128)(2,1)}, u32[]{:S(2)}) copy-start(bf16[4,6,16,384]{3,2,1,0:T(8,128)(2,1)} %param.5) | copy-start | bytes 884740
  1.9 1.0 %copy-start.2 = (bf16[4,6,16,384]{3,2,1,0:T(8,128)(2,1)S(1)}, bf16[4,6,16,384]{3,2,1,0:T(8,128)(2,1)}, u32[]{:S(2)}) copy-start(bf16[4,6,16,384]{3,2,1,0:T(8,128)(2,1)} %param.6) | copy-start | bytes 884740
  2.9 0.8 %copy-start.3 = (s32[64,64]{1,0:T(8,128)S(1)}, s32[64,64]{1,0:T(8,128)}, u32[]{:S(2)}) copy-start(s32[64,64]{1,0:T(8,128)} %mask_ref.1) | copy-start | bytes 49156

commit v2 on v1

v2 whole, which is shorter than its diff:
```python
import functools

import jax
import jax.numpy as jnp
from jax import lax
from jax.experimental import pallas as pl
from jax.experimental.pallas import tpu as pltpu
from jax.sharding import PartitionSpec as P

HEAD_DIM = 128
TILE_T = 4
TILE_R = 6
TILE_C = 8
MESH = pl.DeviceIdType.MESH
NEG_FILL = -1e30
EXP_SCALE = HEAD_DIM**-0.5 * 1.4426950408889634
NT = (((1,), (1,)), ((), ()))
FLOOR = -1e29
OFFSETS = (0, 3, 1, 2)
ORDER = (
    (0, 0, 0), (0, 1, 0), (0, 0, 1), (1, 0, 0), (1, 1, 0), (0, 1, 1),
    (1, 0, 1), (2, 0, 0), (2, 1, 0), (1, 1, 1), (2, 0, 1), (2, 1, 1),
)


def kernel(
    heads, tok,
    q_in, k_in, v_in, mask_ref, out_ref,
    qbuf, kbuf, vbuf, v_own, mask, vt, bias, peak, acc, osend, orecv, done, load_s,
    swap_s, swap_r, x_s, x_r, d_s, d_r, q_s, q_r, o_s, o_r, f_s, f_r,
):
    head = lax.axis_index("head")
    tm = lax.axis_index("tm")
    y = lax.axis_index("height")
    nx = lax.axis_size("tm") // 2
    ny = lax.axis_size("height")
    zh, c = lax.div(head, 2), lax.rem(head, 2)
    x, z = lax.div(tm, 2), lax.rem(tm, 2)
    same = c == z
    inner = jnp.logical_and(y > 0, y < ny - 1)
    own_t = 2 * x + c

    def dev(h, t, r):
        return {"head": h, "tm": t, "height": r}

    partner_head, partner_tm = 2 * zh + z, 2 * x + c
    partner = dev(partner_head, partner_tm, y)
    right = dev(head, 2 * lax.rem(x + 1, nx) + z, y)
    left = dev(head, 2 * lax.rem(x + nx - 1, nx) + z, y)
    sibling = dev(2 * zh + 1 - c, tm, y)

    def remote(src, dst, ssem, rsem, to):
        return pltpu.make_async_remote_copy(
            src_ref=src, dst_ref=dst, send_sem=ssem, recv_sem=rsem, device_id=to, device_id_type=MESH
        )

    barrier = pltpu.get_barrier_semaphore()

    def greet(to):
        pl.semaphore_signal(barrier, inc=1, device_id=to, device_id_type=MESH)

    greet(right)
    greet(left)
    greet(sibling)
    pl.when(y > 0)(lambda: greet(dev(head, tm, y - 1)))
    pl.when(y < ny - 1)(lambda: greet(dev(head, tm, y + 1)))

    pl.when(jnp.logical_not(same))(lambda: greet(partner))

    load_v = pltpu.make_async_copy(v_in, v_own, load_s.at[0])
    load_mask = pltpu.make_async_copy(mask_ref, mask, load_s.at[1])
    load_v.start()
    load_mask.start()

    per_edge = (y > 0).astype(jnp.int32) + (y < ny - 1).astype(jnp.int32)
    pl.semaphore_wait(barrier, 3 + per_edge + jnp.where(same, 0, 1))

    def prepare():
        for h in range(heads):
            acc[h] = jnp.zeros(acc.shape[1:], jnp.float32)
            peak[h] = jnp.full(peak.shape[1:], FLOOR, jnp.float32)
            for t in range(2 * nx):
                vbuf[h, t, HEAD_DIM:] = jnp.ones((16, tok), jnp.bfloat16)
        load_mask.wait()
        row_tiles = ny
        tiles = mask.shape[0]
        key_row = lax.broadcasted_iota(jnp.int32, (4 * nx, tiles), 0)
        key_tile = (lax.shift_right_logical(key_row, 1) * row_tiles + y) * 2 + (key_row & 1)
        key_hot = (lax.broadcasted_iota(jnp.int32, (4 * nx, tiles), 1) == key_tile).astype(jnp.bfloat16)
        by_key = lax.dot_general(
            key_hot, mask[...].astype(jnp.float32).astype(jnp.bfloat16), NT, preferred_element_type=jnp.float32
        ).astype(jnp.bfloat16)
        col = lax.broadcasted_iota(jnp.int32, (1, tok), 1)
        col_tile = lax.shift_right_logical(col, 3) & 1
        tile_id = lax.broadcasted_iota(jnp.int32, (tiles, tok), 0)
        for b in range(3):
            q_tile = (own_t * row_tiles + q_rows[b]) * 2 + col_tile
            q_hot = (tile_id == q_tile).astype(jnp.bfloat16)
            live = jnp.dot(by_key, q_hot, preferred_element_type=jnp.float32)
            fill = (1.0 - live) * NEG_FILL
            for i in range(4 * nx):
                bias[i // 2, 8 * (i % 2) : 8 * (i % 2) + 8, b * tok : (b + 1) * tok] = jnp.broadcast_to(
                    fill[i : i + 1], (8, tok)
                )

    q_rows = (y, jnp.where(y > 0, y - 1, y + 1), y + 1)

    def swap_parts(h):
        cols = slice(h * HEAD_DIM, (h + 1) * HEAD_DIM)
        return (
            (q_in.at[:, cols], lambda t: qbuf.at[h, pl.ds(0, tok)]),
            (k_in.at[:, cols], lambda t: kbuf.at[h, t]),
            (vt.at[h], lambda t: vbuf.at[h, t, pl.ds(0, HEAD_DIM)]),
        )

    def swap_start(h, i):
        src, dst = swap_parts(h)[i]

        @pl.when(same)
        def _():
            pltpu.make_async_copy(src, dst(own_t), swap_r.at[h, i]).start()

        @pl.when(jnp.logical_not(same))
        def _():
            remote(src, dst(2 * x + z), swap_s.at[h, i], swap_r.at[h, i], partner).start()

    def swap_wait(h, i):
        src = (qbuf.at[h, pl.ds(0, tok)], kbuf.at[h, own_t], vbuf.at[h, own_t, pl.ds(0, HEAD_DIM)])[i]

        @pl.when(same)
        def _():
            pltpu.make_async_copy(src, src, swap_r.at[h, i]).wait()

        @pl.when(jnp.logical_not(same))
        def _():
            remote(src, src, swap_s.at[h, i], swap_r.at[h, i], partner).wait_recv()

    def block(d):
        return lax.rem(x + OFFSETS[d], nx)

    def slot(d):
        return 2 * block(d) + c

    def piece(h, kind, t):
        return kbuf.at[h, t] if kind == 0 else vbuf.at[h, t, pl.ds(0, HEAD_DIM)]

    def x_copy(h, direction, step, kind, d, src=None):
        ref = piece(h, kind, slot(d))
        return remote(
            ref if src is None else src, ref, x_s.at[h, direction, step], x_r.at[h, direction, step], right if direction == 0 else left
        )

    def d_copy(h, kind, d, mine=True, src=None):
        t = slot(d) if mine else 2 * block(d) + 1 - c
        ref = piece(h, kind, t)
        return remote(ref if src is None else src, ref, d_s.at[h, d, kind], d_r.at[h, d, kind], sibling)

    def q_copies(h, act, src=None):
        src = qbuf.at[h, pl.ds(0, tok)] if src is None else src

        @pl.when(y < ny - 1)
        def _():
            act(remote(src, qbuf.at[h, pl.ds(tok, tok)], q_s.at[h, 0], q_r.at[h, 0], dev(head, tm, y + 1)))

        @pl.when(y > 0)
        def _():
            at = pl.multiple_of(jnp.where(y > 1, 2 * tok, tok), tok)
            act(remote(src, qbuf.at[h, pl.ds(at, tok)], q_s.at[h, 1], q_r.at[h, 1], dev(head, tm, y - 1)))

    def q_wait(h):
        @pl.when(y > 0)
        def _():
            ref = qbuf.at[h, pl.ds(tok, tok)]
            remote(ref, ref, q_s.at[h, 0], q_r.at[h, 0], dev(head, tm, y - 1)).wait_recv()

        @pl.when(y < ny - 1)
        def _():
            at = pl.multiple_of(jnp.where(y > 0, 2 * tok, tok), tok)
            ref = qbuf.at[h, pl.ds(at, tok)]
            remote(ref, ref, q_s.at[h, 1], q_r.at[h, 1], dev(head, tm, y + 1)).wait_recv()

    def send_part(h, i, src=None):
        if i == 0:
            q_copies(h, lambda copy: copy.start(), src)
        else:
            kind = i - 1
            x_copy(h, 0, kind, kind, 0, src).start()
            x_copy(h, 1, kind, kind, 0, src).start()
            d_copy(h, kind, 0, True, src).start()

    def begin(h, i):
        if (h, i) == (0, 2):
            load_v.wait()
        if i == 2:
            vt[h] = v_own[:, h * HEAD_DIM : (h + 1) * HEAD_DIM].astype(jnp.float32).T.astype(jnp.bfloat16)
        swap_start(h, i)
        if h < 2:
            pl.when(same)(lambda: send_part(h, i, swap_parts(h)[i][0]))

    def own_part(h, i):
        swap_wait(h, i)
        if h < 2:
            pl.when(jnp.logical_not(same))(lambda: send_part(h, i))
        else:
            send_part(h, i)

    def pass_on(h):
        x_copy(h, 0, 0, 0, 1).wait_recv()
        x_copy(h, 0, 2, 0, 1).start()
        d_copy(h, 0, 1).start()
        x_copy(h, 1, 0, 0, 2).wait_recv()
        d_copy(h, 0, 2).start()
        x_copy(h, 1, 1, 1, 2).wait_recv()
        x_copy(h, 1, 2, 1, 2).start()
        d_copy(h, 1, 2).start()
        x_copy(h, 0, 1, 1, 1).wait_recv()
        d_copy(h, 1, 1).start()

    def take_last(h):
        x_copy(h, 0, 2, 0, 3).wait_recv()
        d_copy(h, 0, 3).start()
        x_copy(h, 1, 2, 1, 3).wait_recv()
        d_copy(h, 1, 3).start()

    def unit(h, pair, e):
        @pl.when(jnp.logical_not(same) if e == 0 else same)
        def _():
            for i in range(2):
                d_copy(h, 0, 2 * pair + i, False).wait_recv()
                d_copy(h, 1, 2 * pair + i, False).wait_recv()

        parity = z if e == 0 else 1 - z
        times = [2 * block(2 * pair + i) + parity for i in range(2)]
        state = {}

        def scores(n):
            cols = slice(n * tok, (n + 1) * tok)
            halves, tops = [], []
            for t in times:
                s = lax.dot_general(kbuf[h, t], qbuf[h, cols], NT, preferred_element_type=jnp.float32)
                s = s.reshape(tok // 16, 16, tok)
                halves.append(s)
                tops.append(jnp.max(s, axis=0) + bias[t, :, cols])
            top = jnp.max(jnp.maximum(tops[0], tops[1]), axis=0, keepdims=True)
            before = peak[h, :1, cols]
            top = jnp.maximum(before, top)
            state["fade", n] = jnp.exp2((before - top) * EXP_SCALE)
            peak[h, :1, cols] = top
            state["s", n] = halves
            state["top", n] = top

        def weigh(n):
            cols = slice(n * tok, (n + 1) * tok)
            parts = []
            for t, s in zip(times, state.pop(("s", n))):
                shift = (bias[t, :, cols] - state["top", n]) * EXP_SCALE
                parts.append(jnp.exp2(s * EXP_SCALE + shift[None]).reshape(tok, tok).astype(jnp.bfloat16))
            state["w", n] = jnp.concatenate(parts, axis=0)

        def gather(n):
            cols = slice(n * tok, (n + 1) * tok)
            values = jnp.concatenate([vbuf[h, t] for t in times], axis=1)
            o = jnp.dot(values, state.pop(("w", n)), preferred_element_type=jnp.float32)
            acc[h, :, cols] = acc[h, :, cols] * state["fade", n] + o

        for n in range(5):
            if n < 3:
                scores(n)
            if n >= 2:
                gather(n - 2)
            if 1 <= n <= 3:
                weigh(n - 1)

    def o_copies(h, act):
        def far(b, row, at):
            return remote(osend.at[h, b], orecv.at[h, at], o_s.at[h, b], o_r.at[h, at], dev(head, tm, row))

        act(far(0, q_rows[1], jnp.where(y > 0, 1, 0)))
        pl.when(inner)(lambda: act(far(1, y + 1, 0)))

    def log_of(h, cols):
        total = jnp.maximum(acc[h, HEAD_DIM : HEAD_DIM + 1, cols], 1e-30)
        return total, peak[h, :1, cols] * EXP_SCALE + jnp.log2(total)

    def finish(h):
        row = lax.broadcasted_iota(jnp.int32, (16, tok), 0)
        for b in (1, 2):
            cols = slice(b * tok, (b + 1) * tok)
            total, log = log_of(h, cols)
            osend[h, b - 1, :HEAD_DIM] = (acc[h, :HEAD_DIM, cols] * (1.0 / total)).astype(jnp.bfloat16)
            hi = log.astype(jnp.bfloat16).astype(jnp.float32)
            mid = (log - hi).astype(jnp.bfloat16).astype(jnp.float32)
            low = log - hi - mid
            osend[h, b - 1, HEAD_DIM:] = jnp.where(row == 0, hi, jnp.where(row == 1, mid, low)).astype(jnp.bfloat16)
        o_copies(h, lambda copy: copy.start())

    def out_cols(h):
        return out_ref.at[:, h * HEAD_DIM : (h + 1) * HEAD_DIM]

    def merge(h):
        def far(at, row):
            ref = orecv.at[h, at]
            remote(ref, ref, o_s.at[h, 0], o_r.at[h, at], dev(head, tm, row)).wait_recv()

        pl.when(y > 0)(lambda: far(0, y - 1))
        pl.when(y < ny - 1)(lambda: far(1, y + 1))
        there = (y > 0, y < ny - 1)
        total, log = log_of(h, slice(0, tok))
        logs, parts = [log], [acc[h, :HEAD_DIM, :tok]]
        for at in range(2):
            tail = orecv[h, at, HEAD_DIM:].astype(jnp.float32)
            logs.append(jnp.where(there[at], tail[0:1] + tail[1:2] + tail[2:3], -3e38))
            parts.append(jnp.where(there[at], orecv[h, at, :HEAD_DIM].astype(jnp.float32), 0.0))
        top = jnp.maximum(jnp.maximum(logs[0], logs[1]), logs[2])
        shares = [jnp.exp2(log - top) for log in logs]
        scale = 1.0 / (shares[0] + shares[1] + shares[2])
        shares[0] = shares[0] / total
        result = sum(part * (share * scale) for part, share in zip(parts, shares))
        done[h] = result.T.astype(jnp.bfloat16)

        @pl.when(same)
        def _():
            pltpu.make_async_copy(done.at[h], out_cols(h), f_r.at[h]).start()

        @pl.when(jnp.logical_not(same))
        def _():
            remote(done.at[h], out_cols(h), f_s.at[h], f_r.at[h], partner).start()

    for h in range(heads):
        for i in range(3):
            begin(h, i)
    prepare()
    for i in range(3):
        own_part(0, i)

    events_same = {
        0: [(q_wait, 0), (pass_on, 0), (own_part, 2, 0), (own_part, 2, 1), (own_part, 2, 2)],
        1: [(pass_on, 1), (take_last, 0)],
        2: [(own_part, 1, 0), (own_part, 1, 1), (own_part, 1, 2)],
        3: [(q_wait, 1), (pass_on, 2)],
        4: [(take_last, 1)],
        7: [(q_wait, 2), (take_last, 2)],
    }
    events_swapped = {
        0: [(q_wait, 0), (own_part, 1, 0)],
        1: [(own_part, 1, 1), (own_part, 1, 2)],
        2: [(pass_on, 0)],
        3: [(own_part, 2, 0), (q_wait, 1)],
        4: [(own_part, 2, 1), (pass_on, 1)],
        5: [(own_part, 2, 2), (take_last, 0)],
        7: [(q_wait, 2), (pass_on, 2)],
        8: [(take_last, 1)],
        11: [(take_last, 2)],
    }
    last_of = {h: max(i for i, (g, _, _) in enumerate(ORDER) if g == h) for h in range(heads)}

    for n, (h, pair, e) in enumerate(ORDER):
        for table, role in ((events_same, same), (events_swapped, jnp.logical_not(same))):

            @pl.when(role)
            def _(acts=table.get(n, ())):
                for act, *which in acts:
                    act(*which)

        unit(h, pair, e)
        if n == last_of[h]:
            finish(h)
        for g in range(heads - 1):
            if n == last_of[g] + 2:
                merge(g)

    merge(heads - 1)
    for h in range(heads):

        @pl.when(same)
        def _(h=h):
            pltpu.make_async_copy(done.at[h], out_cols(h), f_r.at[h]).wait()

        @pl.when(jnp.logical_not(same))
        def _(h=h):
            copy = remote(done.at[h], out_cols(h), f_s.at[h], f_r.at[h], partner)
            copy.wait_send()
            copy.wait_recv()

    def drain(h, carry):
        @pl.when(jnp.logical_not(same))
        def _():
            for i, (src, dst) in enumerate(
                ((qbuf.at[h, pl.ds(0, tok)], 0), (kbuf.at[h, 0], 0), (vt.at[h], 0))
            ):
                remote(src, src, swap_s.at[h, i], swap_r.at[h, i], partner).wait_send()

        for direction in range(2):
            x_copy(h, direction, 0, 0, 0).wait_send()
            x_copy(h, direction, 1, 1, 0).wait_send()
        x_copy(h, 0, 2, 0, 1).wait_send()
        x_copy(h, 1, 2, 1, 2).wait_send()
        for d in range(4):
            d_copy(h, 0, d).wait_send()
            d_copy(h, 1, d).wait_send()
        q_copies(h, lambda copy: copy.wait_send())
        o_copies(h, lambda copy: copy.wait_send())
        return carry

    lax.fori_loop(0, heads, drain, 0)


def solution(mesh):
    times = mesh.shape["tm"]

    def shards(queries, key_tokens, value_tokens, tile_mask):
        frames, rows, cols, chans = queries.shape
        tok = frames * rows * cols
        heads = chans // HEAD_DIM
        bf16, f32 = jnp.bfloat16, jnp.float32
        dma = pltpu.SemaphoreType.DMA
        out = pl.pallas_call(
            functools.partial(kernel, heads, tok),
            out_shape=jax.ShapeDtypeStruct((tok, chans), bf16),
            in_specs=[pl.BlockSpec(memory_space=pl.ANY)] * 4,
            out_specs=pl.BlockSpec(memory_space=pl.ANY),
            scratch_shapes=[
                pltpu.VMEM((heads, 3 * tok, HEAD_DIM), bf16),
                pltpu.VMEM((heads, times, tok, HEAD_DIM), bf16),
                pltpu.VMEM((heads, times, HEAD_DIM + 16, tok), bf16),
                pltpu.VMEM((tok, chans), bf16),
                pltpu.VMEM(tile_mask.shape, jnp.int32),
                pltpu.VMEM((heads, HEAD_DIM, tok), bf16),
                pltpu.VMEM((times, 16, 3 * tok), f32),
                pltpu.VMEM((heads, 8, 3 * tok), f32),
                pltpu.VMEM((heads, HEAD_DIM + 16, 3 * tok), f32),
                pltpu.VMEM((heads, 2, HEAD_DIM + 16, tok), bf16),
                pltpu.VMEM((heads, 2, HEAD_DIM + 16, tok), bf16),
                pltpu.VMEM((heads, tok, HEAD_DIM), bf16),
                dma((2,)),
                dma((heads, 3)), dma((heads, 3)),
                dma((heads, 2, 3)), dma((heads, 2, 3)),
                dma((heads, 4, 2)), dma((heads, 4, 2)),
                dma((heads, 2)), dma((heads, 2)),
                dma((heads, 2)), dma((heads, 2)),
                dma((heads,)), dma((heads,)),
            ],
            compiler_params=pltpu.CompilerParams(
                collective_id=0, has_side_effects=True, vmem_limit_bytes=60 * 2**20
            ),
        )(
            queries.reshape(tok, chans),
            key_tokens.reshape(tok, chans),
            value_tokens.reshape(tok, chans),
            tile_mask,
        )
        return out.reshape(frames, rows, cols, chans)

    return jax.shard_map(
        shards,
        mesh=mesh,
        in_specs=(
            P("tm", "height", None, "head"),
            P("tm", "height", None, "head"),
            P("tm", "height", None, "head"),
            P(),
        ),
        out_specs=P("tm", "height", None, "head"),
        check_vma=False,
    )
```

time: 51.6 us -> 45 us (0.87)
  Pallas kernels: 46.5 us -> 43.1 us
  local copies, waits for them, and re-layouts: 4.86 us -> 1.71 us
    pallas_call x1, Pallas kernels: 46.5 us -> 43.1 us  [shards(): pl.pallas_call(functools.partial(kernel, heads, tok), out_shape=jax.Shape...]
    unnamed x8 -> x1, local copies, waits for them, and re-layouts: 3.64 us -> 1.71 us
    reshape x1 -> x0, local copies, waits for them, and re-layouts: 0.97 us -> none  [shards(): return jnp.transpose(out, (1, 0, 2)).reshape(frames, rows, cols, chans)]
where the time goes in v2:
time: 45 us; the launch traced here: 44.8 us
  Pallas kernels  43.1 us (96%)
  local copies, waits for them, and re-layouts  1.71 us (4%)
    pallas_call x1, Pallas kernels, shards(): pl.pallas_call(functools.partial(kernel, heads, tok), out_shape=jax.Shape...  43.1 us
    unnamed x1, local copies, waits for them, and re-layouts  1.71 us

profile of v2, /device:TPU:1, one launch (start us, length us, event | category | flops | bytes accessed | tf_op | source)
XLA Modules:
  0.0 44.8 jit_solution(13039903544378047790)
XLA Ops:
  0.0 43.1 %shard_map.46 = bf16[384,384]{1,0:T(8,128)(2,1)} custom-call(bf16[384,384]{1,0:T(8,128)(2,1)} %bitcast.5, bf16[384,384]{1,0:T(8,128)(2,1)} %bitcast.6, bf16[384,384]{1,0:T(8,128)(2,1)} %bitcast.7, s32[64,64]{1,0:T(8,128)} %mask_ref.1), custom_call_target="tpu_custom_call" | custom-call | tf_op jit(solution)/shard_map/pallas_call | solution.py:417
  43.1 1.7 %copy.6 = bf16[4,6,16,384]{3,2,1,0:T(8,128)(2,1)} copy(bf16[4,6,16,384]{3,2,1,0:T(8,128)(2,1)} %bitcast.4) | data formatting | bytes 589824

commit v3 on v2

--- a/solution.py
+++ b/solution.py
@@ -17,10 +17,7 @@
 NT = (((1,), (1,)), ((), ()))
 FLOOR = -1e29
 OFFSETS = (0, 3, 1, 2)
-ORDER = (
-    (0, 0, 0), (0, 1, 0), (0, 0, 1), (1, 0, 0), (1, 1, 0), (0, 1, 1),
-    (1, 0, 1), (2, 0, 0), (2, 1, 0), (1, 1, 1), (2, 0, 1), (2, 1, 1),
-)
+OWN, NEAR = ((0, 256), (256, 384)), ((384, 640), (640, 896), (896, 1152))
 
 
 def kernel(
@@ -222,53 +219,59 @@
         x_copy(h, 1, 2, 1, 3).wait_recv()
         d_copy(h, 1, 3).start()
 
-    def unit(h, pair, e):
-        @pl.when(jnp.logical_not(same) if e == 0 else same)
-        def _():
-            for i in range(2):
-                d_copy(h, 0, 2 * pair + i, False).wait_recv()
-                d_copy(h, 1, 2 * pair + i, False).wait_recv()
-
-        parity = z if e == 0 else 1 - z
-        times = [2 * block(2 * pair + i) + parity for i in range(2)]
+    def work(units):
+        for e in range(2):
+            pieces = [(h, 2 * pair + i) for _, h, pair, g in units if g == e for i in range(2)]
+            pieces = [piece for piece in pieces if (piece, e) not in taken]
+            taken.update((piece, e) for piece in pieces)
+
+            @pl.when(jnp.logical_not(same) if e == 0 else same)
+            def _(pieces=pieces):
+                for h, d in pieces:
+                    d_copy(h, 0, d, False).wait_recv()
+                    d_copy(h, 1, d, False).wait_recv()
+
+        tasks = [(h, pair, e, slice(*cols)) for columns, h, pair, e in units for cols in columns]
         state = {}
 
+        def times(pair, e):
+            return [2 * block(2 * pair + i) + (z if e == 0 else 1 - z) for i in range(2)]
+
         def scores(n):
-            cols = slice(n * tok, (n + 1) * tok)
-            halves, tops = [], []
-            for t in times:
+            h, pair, e, cols = tasks[n]
+            parts, tops = [], []
+            for t in times(pair, e):
                 s = lax.dot_general(kbuf[h, t], qbuf[h, cols], NT, preferred_element_type=jnp.float32)
-                s = s.reshape(tok // 16, 16, tok)
-                halves.append(s)
+                s = s.reshape(tok // 16, 16, -1)
+                parts.append(s)
                 tops.append(jnp.max(s, axis=0) + bias[t, :, cols])
             top = jnp.max(jnp.maximum(tops[0], tops[1]), axis=0, keepdims=True)
             before = peak[h, :1, cols]
             top = jnp.maximum(before, top)
-            state["fade", n] = jnp.exp2((before - top) * EXP_SCALE)
             peak[h, :1, cols] = top
-            state["s", n] = halves
-            state["top", n] = top
+            state[n] = parts, top, jnp.exp2((before - top) * EXP_SCALE)
 
         def weigh(n):
-            cols = slice(n * tok, (n + 1) * tok)
-            parts = []
-            for t, s in zip(times, state.pop(("s", n))):
-                shift = (bias[t, :, cols] - state["top", n]) * EXP_SCALE
-                parts.append(jnp.exp2(s * EXP_SCALE + shift[None]).reshape(tok, tok).astype(jnp.bfloat16))
-            state["w", n] = jnp.concatenate(parts, axis=0)
+            h, pair, e, cols = tasks[n]
+            parts, top, fade = state[n]
+            weights = []
+            for t, s in zip(times(pair, e), parts):
+                shift = (bias[t, :, cols] - top) * EXP_SCALE
+                weights.append(jnp.exp2(s * EXP_SCALE + shift[None]).reshape(tok, -1).astype(jnp.bfloat16))
+            state[n] = jnp.concatenate(weights, axis=0), fade
 
         def gather(n):
-            cols = slice(n * tok, (n + 1) * tok)
-            values = jnp.concatenate([vbuf[h, t] for t in times], axis=1)
-            o = jnp.dot(values, state.pop(("w", n)), preferred_element_type=jnp.float32)
-            acc[h, :, cols] = acc[h, :, cols] * state["fade", n] + o
-
-        for n in range(5):
-            if n < 3:
+            h, pair, e, cols = tasks[n]
+            weights, fade = state.pop(n)
+            values = jnp.concatenate([vbuf[h, t] for t in times(pair, e)], axis=1)
+            acc[h, :, cols] = acc[h, :, cols] * fade + jnp.dot(values, weights, preferred_element_type=jnp.float32)
+
+        for n in range(len(tasks) + 2):
+            if n < len(tasks):
                 scores(n)
             if n >= 2:
                 gather(n - 2)
-            if 1 <= n <= 3:
+            if 1 <= n <= len(tasks):
                 weigh(n - 1)
 
     def o_copies(h, act):
@@ -326,50 +329,50 @@
         def _():
             remote(done.at[h], out_cols(h), f_s.at[h], f_r.at[h], partner).start()
 
-    for h in range(heads):
-        for i in range(3):
-            begin(h, i)
+    for h, i in [(h, i) for h in range(2) for i in range(3)] + [(2, 1), (2, 2), (2, 0)]:
+        begin(h, i)
     prepare()
     for i in range(3):
         own_part(0, i)
 
-    events_same = {
-        0: [(q_wait, 0), (pass_on, 0), (own_part, 2, 0), (own_part, 2, 1), (own_part, 2, 2)],
-        1: [(pass_on, 1), (take_last, 0)],
-        2: [(own_part, 1, 0), (own_part, 1, 1), (own_part, 1, 2)],
-        3: [(q_wait, 1), (pass_on, 2)],
-        4: [(take_last, 1)],
-        7: [(q_wait, 2), (take_last, 2)],
-    }
-    events_swapped = {
-        0: [(q_wait, 0), (own_part, 1, 0)],
-        1: [(own_part, 1, 1), (own_part, 1, 2)],
-        2: [(pass_on, 0)],
-        3: [(own_part, 2, 0), (q_wait, 1)],
-        4: [(own_part, 2, 1), (pass_on, 1)],
-        5: [(own_part, 2, 2), (take_last, 0)],
-        7: [(q_wait, 2), (pass_on, 2)],
-        8: [(take_last, 1)],
-        11: [(take_last, 2)],
-    }
-    last_of = {h: max(i for i, (g, _, _) in enumerate(ORDER) if g == h) for h in range(heads)}
-
-    for n, (h, pair, e) in enumerate(ORDER):
-        for table, role in ((events_same, same), (events_swapped, jnp.logical_not(same))):
-
-            @pl.when(role)
-            def _(acts=table.get(n, ())):
-                for act, *which in acts:
-                    act(*which)
-
-        unit(h, pair, e)
-        if n == last_of[h]:
-            finish(h)
-        for g in range(heads - 1):
-            if n == last_of[g] + 2:
-                merge(g)
-
-    merge(heads - 1)
+    taken = set()
+    steps = [
+        ([(pass_on, 0)], [], [(OWN, 0, 0, 0)], []),
+        (
+            [(own_part, 2, 0), (own_part, 2, 1), (own_part, 2, 2), (pass_on, 1)]
+            + [(own_part, 1, i) for i in range(3)]
+            + [(q_wait, 0)],
+            [(own_part, 1, 0), (own_part, 1, 1), (q_wait, 0)],
+            [(NEAR, 0, 0, 0), (OWN, 1, 0, 0)],
+            [],
+        ),
+        ([(take_last, 0)], [(own_part, 1, 2), (own_part, 2, 1)], [(NEAR, 0, 1, 0)], []),
+        (
+            [(q_wait, 1)],
+            [(pass_on, 0), (own_part, 2, 2), (own_part, 2, 0), (q_wait, 1)],
+            [(NEAR, 0, 0, 1), (NEAR, 1, 0, 0)],
+            [],
+        ),
+        ([(pass_on, 2), (take_last, 1)], [], [(OWN, 0, 1, 0), (OWN, 0, 0, 1)], []),
+        ([(q_wait, 2)], [(pass_on, 1), (q_wait, 2)], [(NEAR, 2, 0, 0), (NEAR, 1, 0, 1)], []),
+        ([(take_last, 2)], [(take_last, 0)], [(NEAR, 1, 1, 0), (NEAR, 0, 1, 1)], [(finish, 0)]),
+        ([], [(pass_on, 2), (take_last, 1)], [(NEAR, 1, 1, 1), (NEAR, 2, 1, 0)], [(finish, 1)]),
+        ([], [], [(OWN, 0, 1, 1), (OWN, 1, 1, 0), (NEAR, 2, 0, 1)], []),
+        ([], [(take_last, 2)], [(NEAR, 2, 1, 1)], [(finish, 2)]),
+        ([], [], [(OWN, 1, 0, 1), (OWN, 1, 1, 1)], [(merge, 0)]),
+        ([], [], [(OWN, 2, 0, 0), (OWN, 2, 1, 0), (OWN, 2, 0, 1), (OWN, 2, 1, 1)], [(merge, 1), (merge, 2)]),
+    ]
+
+    def do(acts):
+        for act, *which in acts:
+            act(*which)
+
+    for acts_same, acts_swapped, units, acts_then in steps:
+        pl.when(same)(lambda: do(acts_same))
+        pl.when(jnp.logical_not(same))(lambda: do(acts_swapped))
+        work(units)
+        do(acts_then)
+
     for h in range(heads):
 
         @pl.when(same)

time: 45 us -> 40.6 us (0.902)
  Pallas kernels: 43.1 us -> 38.8 us
    pallas_call x1, Pallas kernels: 43.1 us -> 38.8 us  [shards(): pl.pallas_call(functools.partial(kernel, heads, tok), out_shape=jax.Shape...]
where the time goes in v3:
time: 40.6 us; the launch traced here: 40.5 us
  Pallas kernels  38.8 us (96%)
  local copies, waits for them, and re-layouts  1.71 us (4%)
    pallas_call x1, Pallas kernels, shards(): pl.pallas_call(functools.partial(kernel, heads, tok), out_shape=jax.Shape...  38.8 us
    unnamed x1, local copies, waits for them, and re-layouts  1.71 us

profile of v3, /device:TPU:1, one launch (start us, length us, event | category | flops | bytes accessed | tf_op | source)
XLA Modules:
  0.0 40.5 jit_solution(5671175189798189498)
XLA Ops:
  0.0 38.8 %shard_map.46 = bf16[384,384]{1,0:T(8,128)(2,1)} custom-call(bf16[384,384]{1,0:T(8,128)(2,1)} %bitcast.5, bf16[384,384]{1,0:T(8,128)(2,1)} %bitcast.6, bf16[384,384]{1,0:T(8,128)(2,1)} %bitcast.7, s32[64,64]{1,0:T(8,128)} %mask_ref.1), custom_call_target="tpu_custom_call" | custom-call | tf_op jit(solution)/shard_map/pallas_call | solution.py:420
  38.8 1.7 %copy.6 = bf16[4,6,16,384]{3,2,1,0:T(8,128)(2,1)} copy(bf16[4,6,16,384]{3,2,1,0:T(8,128)(2,1)} %bitcast.4) | data formatting | bytes 589824

commit v4 on v3

--- a/solution.py
+++ b/solution.py
@@ -181,9 +181,9 @@
             q_copies(h, lambda copy: copy.start(), src)
         else:
             kind = i - 1
+            d_copy(h, kind, 0, True, src).start()
             x_copy(h, 0, kind, kind, 0, src).start()
             x_copy(h, 1, kind, kind, 0, src).start()
-            d_copy(h, kind, 0, True, src).start()
 
     def begin(h, i):
         if (h, i) == (0, 2):
@@ -203,13 +203,13 @@
 
     def pass_on(h):
         x_copy(h, 0, 0, 0, 1).wait_recv()
+        d_copy(h, 0, 1).start()
         x_copy(h, 0, 2, 0, 1).start()
-        d_copy(h, 0, 1).start()
         x_copy(h, 1, 0, 0, 2).wait_recv()
         d_copy(h, 0, 2).start()
         x_copy(h, 1, 1, 1, 2).wait_recv()
+        d_copy(h, 1, 2).start()
         x_copy(h, 1, 2, 1, 2).start()
-        d_copy(h, 1, 2).start()
         x_copy(h, 0, 1, 1, 1).wait_recv()
         d_copy(h, 1, 1).start()
 
@@ -295,7 +295,10 @@
             mid = (log - hi).astype(jnp.bfloat16).astype(jnp.float32)
             low = log - hi - mid
             osend[h, b - 1, HEAD_DIM:] = jnp.where(row == 0, hi, jnp.where(row == 1, mid, low)).astype(jnp.bfloat16)
-        o_copies(h, lambda copy: copy.start())
+        pl.when(jnp.logical_not(same))(lambda: o_copies(h, lambda copy: copy.start()))
+
+    def finish_same(h):
+        pl.when(same)(lambda: o_copies(h, lambda copy: copy.start()))
 
     def out_cols(h):
         return out_ref.at[:, h * HEAD_DIM : (h + 1) * HEAD_DIM]
@@ -355,12 +358,13 @@
         ),
         ([(pass_on, 2), (take_last, 1)], [], [(OWN, 0, 1, 0), (OWN, 0, 0, 1)], []),
         ([(q_wait, 2)], [(pass_on, 1), (q_wait, 2)], [(NEAR, 2, 0, 0), (NEAR, 1, 0, 1)], []),
-        ([(take_last, 2)], [(take_last, 0)], [(NEAR, 1, 1, 0), (NEAR, 0, 1, 1)], [(finish, 0)]),
-        ([], [(pass_on, 2), (take_last, 1)], [(NEAR, 1, 1, 1), (NEAR, 2, 1, 0)], [(finish, 1)]),
+        ([(take_last, 2)], [(take_last, 0)], [(NEAR, 1, 1, 0), (NEAR, 0, 1, 1)], [(finish, 0), (finish_same, 0)]),
+        ([], [(pass_on, 2), (take_last, 1)], [(NEAR, 1, 1, 1), (NEAR, 2, 1, 0)], [(finish, 1), (finish_same, 1)]),
         ([], [], [(OWN, 0, 1, 1), (OWN, 1, 1, 0), (NEAR, 2, 0, 1)], []),
         ([], [(take_last, 2)], [(NEAR, 2, 1, 1)], [(finish, 2)]),
-        ([], [], [(OWN, 1, 0, 1), (OWN, 1, 1, 1)], [(merge, 0)]),
-        ([], [], [(OWN, 2, 0, 0), (OWN, 2, 1, 0), (OWN, 2, 0, 1), (OWN, 2, 1, 1)], [(merge, 1), (merge, 2)]),
+        ([], [], [(OWN, 1, 0, 1), (OWN, 1, 1, 1)], [(finish_same, 2), (merge, 0)]),
+        ([], [], [(OWN, 2, 0, 0), (OWN, 2, 1, 0)], [(merge, 1)]),
+        ([], [], [(OWN, 2, 0, 1), (OWN, 2, 1, 1)], [(merge, 2)]),
     ]
 
     def do(acts):
@@ -444,7 +448,7 @@
                 dma((heads,)), dma((heads,)),
             ],
             compiler_params=pltpu.CompilerParams(
-                collective_id=0, has_side_effects=True, vmem_limit_bytes=60 * 2**20
+                collective_id=0, has_side_effects=True, vmem_limit_bytes=536 * 2**20 // 10
             ),
         )(
             queries.reshape(tok, chans),

time: 40.6 us -> 39.9 us (0.983)
  Pallas kernels: 38.8 us -> 38.2 us
    pallas_call x1, Pallas kernels: 38.8 us -> 38.2 us  [shards(): pl.pallas_call(functools.partial(kernel, heads, tok), out_shape=jax.Shape...]
    unnamed x1 -> x3, local copies, waits for them, and re-layouts: 1.71 us -> 1.47 us
where the time goes in v4:
time: 39.9 us; the launch traced here: 39.7 us
  Pallas kernels  38.2 us (96%)
  local copies, waits for them, and re-layouts  1.47 us (4%)
    pallas_call x1, Pallas kernels, shards(): pl.pallas_call(functools.partial(kernel, heads, tok), out_shape=jax.Shape...  38.2 us
    unnamed x3, local copies, waits for them, and re-layouts  1.47 us

profile of v4, /device:TPU:1, one launch (start us, length us, event | category | flops | bytes accessed | tf_op | source)
XLA Modules:
  0.0 39.7 jit_solution(12590561252951076502)
XLA Ops:
  0.0 0.0 copy-start
  0.0 0.8 %copy-done = s32[64,64]{1,0:T(8,128)S(1)} copy-done((s32[64,64]{1,0:T(8,128)S(1)}, s32[64,64]{1,0:T(8,128)}, u32[]{:S(2)}) %copy-start) | copy-done | bytes 16408
  0.8 38.2 %shard_map.46 = bf16[384,384]{1,0:T(8,128)(2,1)S(1)} custom-call(bf16[384,384]{1,0:T(8,128)(2,1)} %bitcast.5, bf16[384,384]{1,0:T(8,128)(2,1)} %bitcast.6, bf16[384,384]{1,0:T(8,128)(2,1)} %bitcast.7, s32[64,64]{1,0:T(8,128)S(1)} %copy-done), custom_call_target="tpu_custom_call" | custom-call | tf_op jit(solution)/shard_map/pallas_call | solution.py:424
  39.0 0.7 %copy.6 = bf16[4,6,16,384]{3,2,1,0:T(8,128)(2,1)} copy(bf16[4,6,16,384]{3,2,1,0:T(8,128)(2,1)S(1)} %bitcast.4) | data formatting | bytes 589824
Async XLA Ops:
  0.0 0.8 %copy-start = (s32[64,64]{1,0:T(8,128)S(1)}, s32[64,64]{1,0:T(8,128)}, u32[]{:S(2)}) copy-start(s32[64,64]{1,0:T(8,128)} %mask_ref.1) | copy-start | bytes 49156

commit v5 on v4

--- a/solution.py
+++ b/solution.py
@@ -17,6 +17,7 @@
 NT = (((1,), (1,)), ((), ()))
 FLOOR = -1e29
 OFFSETS = (0, 3, 1, 2)
+CHUNKS = ((0, 256), (256, 384))
 OWN, NEAR = ((0, 256), (256, 384)), ((384, 640), (640, 896), (896, 1152))
 
 
@@ -274,12 +275,21 @@
             if 1 <= n <= len(tasks):
                 weigh(n - 1)
 
+    def chunks(h):
+        if h < heads - 1:
+            return ((h, 0, tok),)
+        return tuple((h + i, lo, hi - lo) for i, (lo, hi) in enumerate(CHUNKS))
+
     def o_copies(h, act):
-        def far(b, row, at):
-            return remote(osend.at[h, b], orecv.at[h, at], o_s.at[h, b], o_r.at[h, at], dev(head, tm, row))
-
-        act(far(0, q_rows[1], jnp.where(y > 0, 1, 0)))
-        pl.when(inner)(lambda: act(far(1, y + 1, 0)))
+        for i, lo, width in chunks(h):
+
+            def far(b, row, at, i=i, cols=pl.ds(lo, width)):
+                return remote(
+                    osend.at[h, b, :, cols], orecv.at[h, at, :, cols], o_s.at[i, b], o_r.at[i, at], dev(head, tm, row)
+                )
+
+            act(far(0, q_rows[1], jnp.where(y > 0, 1, 0)))
+            pl.when(inner)(lambda far=far: act(far(1, y + 1, 0)))
 
     def log_of(h, cols):
         total = jnp.maximum(acc[h, HEAD_DIM : HEAD_DIM + 1, cols], 1e-30)
@@ -300,37 +310,39 @@
     def finish_same(h):
         pl.when(same)(lambda: o_copies(h, lambda copy: copy.start()))
 
-    def out_cols(h):
-        return out_ref.at[:, h * HEAD_DIM : (h + 1) * HEAD_DIM]
-
-    def merge(h):
+    def out_copy(h, part, local):
+        i, lo, width = chunks(h)[part]
+        src = done.at[h, pl.ds(lo, width)]
+        dst = out_ref.at[pl.ds(lo, width), h * HEAD_DIM : (h + 1) * HEAD_DIM]
+        if local:
+            return pltpu.make_async_copy(src, dst, f_r.at[i])
+        return remote(src, dst, f_s.at[i], f_r.at[i], partner)
+
+    def merge(h, part=0):
+        i, lo, width = chunks(h)[part]
+        cols = slice(lo, lo + width)
+
         def far(at, row):
-            ref = orecv.at[h, at]
-            remote(ref, ref, o_s.at[h, 0], o_r.at[h, at], dev(head, tm, row)).wait_recv()
+            ref = orecv.at[h, at, :, pl.ds(lo, width)]
+            remote(ref, ref, o_s.at[i, 0], o_r.at[i, at], dev(head, tm, row)).wait_recv()
 
         pl.when(y > 0)(lambda: far(0, y - 1))
         pl.when(y < ny - 1)(lambda: far(1, y + 1))
         there = (y > 0, y < ny - 1)
-        total, log = log_of(h, slice(0, tok))
-        logs, parts = [log], [acc[h, :HEAD_DIM, :tok]]
+        total, log = log_of(h, cols)
+        logs, parts = [log], [acc[h, :HEAD_DIM, cols]]
         for at in range(2):
-            tail = orecv[h, at, HEAD_DIM:].astype(jnp.float32)
+            tail = orecv[h, at, HEAD_DIM:, cols].astype(jnp.float32)
             logs.append(jnp.where(there[at], tail[0:1] + tail[1:2] + tail[2:3], -3e38))
-            parts.append(jnp.where(there[at], orecv[h, at, :HEAD_DIM].astype(jnp.float32), 0.0))
+            parts.append(jnp.where(there[at], orecv[h, at, :HEAD_DIM, cols].astype(jnp.float32), 0.0))
         top = jnp.maximum(jnp.maximum(logs[0], logs[1]), logs[2])
         shares = [jnp.exp2(log - top) for log in logs]
         scale = 1.0 / (shares[0] + shares[1] + shares[2])
         shares[0] = shares[0] / total
         result = sum(part * (share * scale) for part, share in zip(parts, shares))
-        done[h] = result.T.astype(jnp.bfloat16)
-
-        @pl.when(same)
-        def _():
-            pltpu.make_async_copy(done.at[h], out_cols(h), f_r.at[h]).start()
-
-        @pl.when(jnp.logical_not(same))
-        def _():
-            remote(done.at[h], out_cols(h), f_s.at[h], f_r.at[h], partner).start()
+        done[h, cols] = result.T.astype(jnp.bfloat16)
+        pl.when(same)(lambda: out_copy(h, part, True).start())
+        pl.when(jnp.logical_not(same))(lambda: out_copy(h, part, False).start())
 
     for h, i in [(h, i) for h in range(2) for i in range(3)] + [(2, 1), (2, 2), (2, 0)]:
         begin(h, i)
@@ -364,7 +376,7 @@
         ([], [(take_last, 2)], [(NEAR, 2, 1, 1)], [(finish, 2)]),
         ([], [], [(OWN, 1, 0, 1), (OWN, 1, 1, 1)], [(finish_same, 2), (merge, 0)]),
         ([], [], [(OWN, 2, 0, 0), (OWN, 2, 1, 0)], [(merge, 1)]),
-        ([], [], [(OWN, 2, 0, 1), (OWN, 2, 1, 1)], [(merge, 2)]),
+        ([], [], [(OWN, 2, 0, 1), (OWN, 2, 1, 1)], [(merge, 2, 0), (merge, 2, 1)]),
     ]
 
     def do(acts):
@@ -378,16 +390,13 @@
         do(acts_then)
 
     for h in range(heads):
-
-        @pl.when(same)
-        def _(h=h):
-            pltpu.make_async_copy(done.at[h], out_cols(h), f_r.at[h]).wait()
-
-        @pl.when(jnp.logical_not(same))
-        def _(h=h):
-            copy = remote(done.at[h], out_cols(h), f_s.at[h], f_r.at[h], partner)
-            copy.wait_send()
-            copy.wait_recv()
+        for part in range(len(chunks(h))):
+            pl.when(same)(lambda h=h, part=part: out_copy(h, part, True).wait())
+
+            @pl.when(jnp.logical_not(same))
+            def _(h=h, part=part):
+                out_copy(h, part, False).wait_send()
+                out_copy(h, part, False).wait_recv()
 
     def drain(h, carry):
         @pl.when(jnp.logical_not(same))
@@ -406,10 +415,11 @@
             d_copy(h, 0, d).wait_send()
             d_copy(h, 1, d).wait_send()
         q_copies(h, lambda copy: copy.wait_send())
+        return carry
+
+    lax.fori_loop(0, heads, drain, 0)
+    for h in range(heads):
         o_copies(h, lambda copy: copy.wait_send())
-        return carry
-
-    lax.fori_loop(0, heads, drain, 0)
 
 
 def solution(mesh):
@@ -444,8 +454,8 @@
                 dma((heads, 2, 3)), dma((heads, 2, 3)),
                 dma((heads, 4, 2)), dma((heads, 4, 2)),
                 dma((heads, 2)), dma((heads, 2)),
-                dma((heads, 2)), dma((heads, 2)),
-                dma((heads,)), dma((heads,)),
+                dma((heads + 1, 2)), dma((heads + 1, 2)),
+                dma((heads + 1,)), dma((heads + 1,)),
             ],
             compiler_params=pltpu.CompilerParams(
                 collective_id=0, has_side_effects=True, vmem_limit_bytes=536 * 2**20 // 10

time: 39.9 us -> 39.5 us (0.990)
  no operation moved by 1% of the time
where the time goes in v5:
time: 39.5 us; the launch traced here: 39.4 us
  Pallas kernels  37.9 us (96%)
  local copies, waits for them, and re-layouts  1.47 us (4%)
    pallas_call x1, Pallas kernels, shards(): pl.pallas_call(functools.partial(kernel, heads, tok), out_shape=jax.Shape...  37.9 us
    unnamed x3, local copies, waits for them, and re-layouts  1.47 us

profile of v5, /device:TPU:1, one launch (start us, length us, event | category | flops | bytes accessed | tf_op | source)
XLA Modules:
  0.0 39.4 jit_solution(13621298743632190836)
XLA Ops:
  0.0 0.0 copy-start
  0.0 0.8 %copy-done = s32[64,64]{1,0:T(8,128)S(1)} copy-done((s32[64,64]{1,0:T(8,128)S(1)}, s32[64,64]{1,0:T(8,128)}, u32[]{:S(2)}) %copy-start) | copy-done | bytes 16408
  0.8 37.9 %shard_map.46 = bf16[384,384]{1,0:T(8,128)(2,1)S(1)} custom-call(bf16[384,384]{1,0:T(8,128)(2,1)} %bitcast.5, bf16[384,384]{1,0:T(8,128)(2,1)} %bitcast.6, bf16[384,384]{1,0:T(8,128)(2,1)} %bitcast.7, s32[64,64]{1,0:T(8,128)S(1)} %copy-done), custom_call_target="tpu_custom_call" | custom-call | tf_op jit(solution)/shard_map/pallas_call | solution.py:434
  38.6 0.7 %copy.6 = bf16[4,6,16,384]{3,2,1,0:T(8,128)(2,1)} copy(bf16[4,6,16,384]{3,2,1,0:T(8,128)(2,1)S(1)} %bitcast.4) | data formatting | bytes 589824
Async XLA Ops:
  0.0 0.8 %copy-start = (s32[64,64]{1,0:T(8,128)S(1)}, s32[64,64]{1,0:T(8,128)}, u32[]{:S(2)}) copy-start(s32[64,64]{1,0:T(8,128)} %mask_ref.1) | copy-start | bytes 49156
